TPU v7x, 32 devices: a whole 2x2x4 slice. The times are simulated.
32 devices in a mesh: grp: 2 (over y), row: 4 (over z), col: 2 (over x), ka: 2 (over core).
Axes of the slice: x: 2, y: 2, z: 4, core: 2. Of those that a mesh axis runs over, the one named last changes fastest.
Arguments:
- left_data: bfloat16 [4, 1024, 32, 256], P('grp', 'row', 'col', 'ka'), parts along dimension 0, may hold values from -6 to 6
- right_data: bfloat16 [4, 32, 256, 1024], P('grp', 'row', 'ka', 'col'), parts along dimension 0, may hold values from -0.125 to 0.125
- taper_table: float32 [8, 256], replicated, may hold values from 0.2 to 1
- pattern: int32 [64, 32], P('row'), may hold values from 0 to 1, as said below
- taper_index: int32 [64, 32], P('row'), may hold values from 0 to 7, as said below
Outputs:
- predicted: float32 [4, 1024, 1024], P('grp', 'row', ('col', 'ka')), parts along dimension 0
There are 2 independent parts, one for each index of `grp`. A program takes and returns all parts, laid end to end along the dimension named above; an argument that names none is the same for every part. Nothing has to cross between parts.
Inputs may be any that keep to these rules, and one draw needn't show every extreme that they name: `pattern`: each receiver block's aperture is one contiguous run of inner blocks around the inner block nearest to it, cut at the ends of the range; its half width varies from block to block, up to 16. `taper_index`: inside an aperture the index grows with the distance from its centre; outside it is 7.
All inputs are finite; a program needn't handle non-finite values.
Results may differ from a plain program's by a relative error of at most 0.0029.
Values may be sent and summed in bfloat16 or wider, within the bound.
A program may use at most 128 MiB of HBM per device.

v0:
```python
import jax
import jax.numpy as jnp
from jax import lax
from jax.sharding import PartitionSpec as P


def blend(left_data, taper_table, pattern, taper_index):
    col_part = left_data.shape[2]
    width = left_data.shape[3]
    rows = left_data.shape[1]
    blocks = pattern.shape[0]
    col_start = lax.axis_index("col") * col_part
    ka_start = lax.axis_index("ka") * width
    used = lax.dynamic_slice_in_dim(pattern, col_start, col_part, 1).astype(jnp.float32)
    levels = lax.dynamic_slice_in_dim(taper_index, col_start, col_part, 1)
    table = lax.dynamic_slice_in_dim(taper_table, ka_start, width, 1)
    onehot = (
        levels[:, :, None] == jnp.arange(taper_table.shape[0], dtype=jnp.int32)[None, None, :]
    ).astype(jnp.float32)
    weights = used[:, :, None] * jnp.einsum(
        "bjt,tw->bjw", onehot, table, precision=lax.Precision.HIGHEST
    )
    shaped = (
        left_data.astype(jnp.float32).reshape(2, blocks, rows // blocks, col_part, width)
        * weights[None, :, None]
    )
    return shaped.reshape(left_data.shape).astype(jnp.bfloat16)


def make_step(panel):

    def contract(piece):
        terms = jnp.einsum("crjw,djws->cdrs", panel, piece, preferred_element_type=jnp.float32)
        return jnp.stack([terms[0, 0] - terms[1, 1], terms[0, 1] + terms[1, 0]])

    def step(carry, piece, start):
        return contract(piece)

    return step


def local(left_data, right_data, taper_table, pattern, taper_index):
    weighted = blend(left_data, taper_table, pattern, taper_index)
    rows = left_data.shape[1]
    halves = lax.all_gather(weighted, "ka", axis=3, tiled=True)
    panel = lax.all_gather(halves, "col", axis=2, tiled=True)
    columns = lax.all_to_all(right_data, "ka", split_axis=3, concat_axis=2, tiled=True)
    start_sum = jnp.zeros((2, rows, columns.shape[3]), jnp.float32)
    result = make_step(panel)(
        start_sum, lax.all_gather(columns, "row", axis=1, tiled=True), jnp.int32(0)
    )
    return result


def solution(mesh):
    placed = (
        P("grp", "row", "col", "ka"),
        P("grp", "row", "ka", "col"),
        P(),
        P("row", None),
        P("row", None),
    )
    return jax.shard_map(
        local, mesh=mesh, in_specs=placed, out_specs=P("grp", "row", ("col", "ka")), check_vma=False
    )
```

profile of v0, /device:TPU:13, one launch (start us, length us, event | category | flops | bytes accessed | tf_op | source)
XLA Modules:
  0.0 297.8 jit_solution(15820236979520449544)
XLA Ops:
  6.5 0.0 copy-start
  6.5 0.0 all-gather.4.cloned.1.call-start
  6.5 0.8 dynamic-slice_convert_fusion
  7.3 0.0 copy-done
  7.3 0.3 convolution_multiply_fusion
  7.7 0.2 mul.31
  7.9 3.6 %multiply_convert_fusion = bf16[2,256,16,128]{3,1,2,0:T(8,128)(2,1)} fusion(bf16[2,256,16,128]{3,2,1,0:T(8,128)(2,1)} %param.5, f32[256,16,128]{2,0,1:T(8,128)S(1)} %bitcast.29), kind=kLoop, calls=%fused_computation.3 | loop fusion | flops 3145728 | bytes 6291456 | tf_op jit(solution)/shard_map/convert_element_type | solution.py:27
  11.5 0.0 copy-start.1
  11.5 0.0 all-gather.4.cloned.1.call-update
  11.5 0.0 all-gather.6.cloned.1.call-start
  11.6 14.9 %all-gather.4.cloned.1.call-done = bf16[2,256,16,256]{3,1,2,0:T(8,128)(2,1)} async-done(((bf16[2,256,16,128]{3,1,2,0:T(8,128)(2,1)}), bf16[2,256,16,256]{3,1,2,0:T(8,128)(2,1)}) %all-gather.4.cloned.1.call-update) | async-done | bytes 4194320 | tf_op jit(solution)/shard_map/all_gather | solution.py:45
  26.5 0.0 all-gather.6.cloned.1.call-update
  26.5 0.0 all-gather.8.cloned.1.call-start
  26.6 0.0 copy-done.1
  26.6 3.1 %copy.11 = bf16[2,8,128,512]{2,1,0,3:T(8,128)(2,1)} copy(bf16[2,8,128,512]{3,2,1,0:T(8,128)(2,1)S(1)} %copy-done.1) | data formatting | bytes 4194304 | tf_op args[1]
  29.7 6.5 %all_to_all.18 = bf16[2,8,128,512]{2,1,0,3:T(8,128)(2,1)S(1)} all-to-all(bf16[2,8,128,512]{2,1,0,3:T(8,128)(2,1)} %copy.11), channel_id=1, replica_groups=mesh['grp'=2,'row'=4,'col'=2,'ka'=2] {'ka'}, dimensions={3} | all-to-all | bytes 4194304 | tf_op jit(solution)/shard_map/all_to_all | solution.py:47
  36.2 2.8 copy.12
  39.0 0.0 all-gather.8.cloned.1.call-update
  39.0 93.5 %all-gather.6.cloned.1.call-done = bf16[2,256,32,256]{3,1,2,0:T(8,128)(2,1)} async-done(((bf16[2,256,16,256]{3,1,2,0:T(8,128)(2,1)}), bf16[2,256,32,256]{3,1,2,0:T(8,128)(2,1)}) %all-gather.6.cloned.1.call-update) | async-done | bytes 8388624 | tf_op jit(solution)/shard_map/all_gather | solution.py:46
  132.5 148.5 %all-gather.8.cloned.1.call-done = bf16[2,32,256,256]{3,2,1,0:T(8,128)(2,1)} async-done(((bf16[2,8,256,256]{3,2,1,0:T(8,128)(2,1)}), bf16[2,32,256,256]{3,2,1,0:T(8,128)(2,1)}) %all-gather.8.cloned.1.call-update) | async-done | bytes 8388624 | tf_op jit(solution)/shard_map/all_gather | solution.py:50
  281.0 9.4 %fusion.3 = f32[2,2,256,256]{3,2,1,0:T(8,128)S(1)} fusion(bf16[2,32,256,256]{3,2,1,0:T(8,128)(2,1)} %all-gather.8.cloned.1.call-done, bf16[2,256,32,256]{3,1,2,0:T(8,128)(2,1)} %all-gather.6.cloned.1.call-done), kind=kOutput, calls=%fused_computation.4 | convolution fusion | flops 4294967296 | bytes 17825792 | tf_op jit(solution)/shard_map/crjw,djws->cdrs/dot_general | solution.py:33
  290.4 0.1 fusion.9
  290.5 0.8 pad_maximum_fusion
  (1 shorter events, 0.0 us)
Async XLA Ops:
  6.5 0.8 copy-start
  6.5 20.0 %all-gather.4.cloned.1.call-start = ((), (), s32[]{:S(2)}) async-start(), calls=%async_computation.1 | async-start | bytes 6291456 | tf_op jit(solution)/shard_map/all_gather | solution.py:45
  11.5 15.1 %copy-start.1 = (bf16[2,8,128,512]{3,2,1,0:T(8,128)(2,1)S(1)}, bf16[2,8,128,512]{3,2,1,0:T(8,128)(2,1)}, u32[]{:S(2)}) copy-start(bf16[2,8,128,512]{3,2,1,0:T(8,128)(2,1)} %param.6) | copy-start | bytes 6291460
  11.5 121.0 %all-gather.6.cloned.1.call-start = ((), (), s32[]{:S(2)}) async-start(), calls=%async_computation.2 | async-start | bytes 12582912 | tf_op jit(solution)/shard_map/all_gather | solution.py:46
  26.5 254.5 %all-gather.8.cloned.1.call-start = ((), (), s32[]{:S(2)}) async-start(), calls=%async_computation.3 | async-start | bytes 10485760 | tf_op jit(solution)/shard_map/all_gather | solution.py:50
Sparse Core Ops, SparseCore 0:
  11.6 14.8 all-gather.3
  28.0 104.4 all-gather.5
  134.1 146.8 all-gather.7
where the time goes:
time: 302 us; the launch traced here: 298 us
  waiting for transfers between devices  257 us (85%)
  between operations  13.2 us (4%)
  matrix products  9.68 us (3%)
  blocking collectives  6.48 us (2%)
  local copies, waits for them, and re-layouts  6.14 us (2%)
  other arithmetic  5.3 us (2%)
    all_gather x1, waiting for transfers between devices, local(): lax.all_gather(columns, 'row', axis=1, tiled=True)  149 us
    all_gather x1, waiting for transfers between devices, local(): panel = lax.all_gather(halves, 'col', axis=2, tiled=True)  93.5 us
    all_gather x1, waiting for transfers between devices, local(): halves = lax.all_gather(weighted, 'ka', axis=3, tiled=True)  14.9 us
    dot_general x1, matrix products, contract(): jnp.einsum('crjw,djws->cdrs', panel, piece, preferred_element_type=jnp.fl...  9.36 us
    all_to_all x1, blocking collectives, local(): lax.all_to_all(right_data, 'ka', split_axis=3, concat_axis=2, tiled=True)  6.48 us
  transfers between devices with their start and end apart: 3, of which 3 were waited for; matrix products, arithmetic and copies ran while one was open for 2% of the time, Pallas kernels for 0%

commit v1 on v0

--- a/solution.py
+++ b/solution.py
@@ -1,6 +1,8 @@
 import jax
 import jax.numpy as jnp
 from jax import lax
+from jax.experimental import pallas as pl
+from jax.experimental.pallas import tpu as pltpu
 from jax.sharding import PartitionSpec as P
 
 
@@ -52,6 +54,261 @@
     return result
 
 
+MESH = pl.DeviceIdType.MESH
+BAND = 32
+OWN, PAIR, EDGE, NEAR = 0, 1, 2, 3
+
+
+def kernel(w_ref, right_ref, out_ref, left, rights, part_out, part_in, send_out, recv_out,
+           loc_sem, pair_sem, near_sem, edge_send, edge_recv, right_send, right_recv,
+           part_send, part_recv, out_send, out_recv):
+    row, col, ka = lax.axis_index("row"), lax.axis_index("col"), lax.axis_index("ka")
+    side = row // 2
+    half = row % 2
+    computes = side == col
+    toward = 1 - 2 * col
+    inner = (row == 1) | (row == 2)
+    depth = left.shape[3]
+    groups = depth // 128
+    rows = left.shape[2]
+    wide = out_ref.shape[2]
+
+    left[EDGE] = jnp.zeros(left.shape[1:], left.dtype)
+
+    barrier = pltpu.get_barrier_semaphore()
+    for step in range(1, 8):
+        to = (row * 2 + col + step) % 8
+        pl.semaphore_signal(barrier, inc=1, device_id={"row": to // 2, "col": to % 2}, device_id_type=MESH)
+    pl.semaphore_signal(barrier, inc=1, device_id={"ka": 1 - ka}, device_id_type=MESH)
+    pl.semaphore_wait(barrier, 8)
+
+    def pair_copy():
+        return pltpu.make_async_remote_copy(
+            w_ref.at[1 - half], left.at[PAIR], pair_sem.at[0], pair_sem.at[1],
+            device_id={"row": 2 * side + 1 - half}, device_id_type=MESH)
+
+    def near_copy(src_half, to_row):
+        return pltpu.make_async_remote_copy(
+            w_ref.at[src_half], left.at[NEAR], near_sem.at[0], near_sem.at[1],
+            device_id={"row": to_row}, device_id_type=MESH)
+
+    def edge_copy(step, below, src_half, to_row):
+        band = pl.ds(BAND * step, BAND)
+        lanes = pl.ds(128 * step, depth - 128 * step) if below else pl.ds(0, 128 * (step + 1))
+        return pltpu.make_async_remote_copy(
+            w_ref.at[src_half, :, band, lanes], left.at[EDGE, :, band, lanes],
+            edge_send.at[step], edge_recv.at[step],
+            device_id={"row": to_row}, device_id_type=MESH)
+
+    def right_copy(order):
+        which = (1 - ka) if order == 0 else ka
+        lanes = pl.ds(pl.multiple_of(which * wide, wide), wide)
+        return pltpu.make_async_remote_copy(
+            right_ref.at[:, :, lanes], rights.at[1, :, :, lanes],
+            right_send.at[order], right_recv.at[order],
+            device_id={"col": 1 - col}, device_id_type=MESH)
+
+    def edges(act):
+        to_row = row - 2 * toward
+        src_half = to_row % 2
+        for below in (True, False):
+            @pl.when(col == (0 if below else 1))
+            def _():
+                for step in range(groups):
+                    act(edge_copy(step, below, src_half, to_row))
+
+    @pl.when(jnp.logical_not(computes))
+    def _():
+        right_copy(0).start()
+        edges(lambda copy: copy.start())
+
+        @pl.when(inner)
+        def _():
+            near_copy(1 - col, row - toward).start()
+
+        right_copy(1).start()
+
+    def own_left():
+        return pltpu.make_async_copy(w_ref.at[half], left.at[OWN], loc_sem.at[0])
+
+    def own_right():
+        return pltpu.make_async_copy(right_ref, rights.at[0], loc_sem.at[1])
+
+    def product(group, sel, which):
+        lanes = pl.ds(pl.multiple_of(which * wide, wide), wide)
+        dot = lambda a, b: jnp.dot(left[group, a], rights[sel, b, :, lanes], preferred_element_type=jnp.float32)
+        return dot(0, 0) - dot(1, 1), dot(0, 1) + dot(1, 0)
+
+    def part_copy(group, sel):
+        return pltpu.make_async_remote_copy(
+            part_out.at[group, sel], part_in.at[group, sel],
+            part_send.at[group, sel], part_recv.at[group, sel],
+            device_id={"ka": 1 - ka}, device_id_type=MESH)
+
+    def row_of(group):
+        pair = row + 1 - 2 * half
+        return jnp.where(group == OWN, row, jnp.where(group == PAIR, pair, jnp.where(
+            group == EDGE, row + 2 * toward, row + toward)))
+
+    def out_copy(group, sel):
+        to_col = col if sel == 0 else 1 - col
+        return pltpu.make_async_remote_copy(
+            send_out.at[group, sel], recv_out.at[row],
+            out_send.at[group, sel], out_recv.at[row],
+            device_id={"row": row_of(group), "col": to_col}, device_id_type=MESH)
+
+    def give(group, sel):
+        real, imag = product(group, sel, 1 - ka)
+        part_out[group, sel, 0] = real
+        part_out[group, sel, 1] = imag
+        part_copy(group, sel).start()
+
+    def keep(group, sel):
+        real, imag = product(group, sel, ka)
+        part_copy(group, sel).wait_recv()
+        real = real + part_in[group, sel, 0]
+        imag = imag + part_in[group, sel, 1]
+
+        def send():
+            send_out[group, sel, 0] = real.astype(jnp.bfloat16)
+            send_out[group, sel, 1] = imag.astype(jnp.bfloat16)
+            out_copy(group, sel).start()
+
+        if sel == 1:
+            send()
+        else:
+            @pl.when(group == OWN)
+            def _():
+                out_ref[0] = real
+                out_ref[1] = imag
+
+            pl.when(group != OWN)(send)
+
+    @pl.when(computes)
+    def _():
+        pair_copy().start()
+        own_left().start()
+        own_right().start()
+        own_left().wait()
+        own_right().wait()
+
+        @pl.loop(0, 2)
+        def _(group):
+            @pl.when(group == PAIR)
+            def _():
+                pair_copy().wait_recv()
+
+            give(group, 0)
+            keep(group, 0)
+
+        right_copy(0).wait_recv()
+
+        @pl.loop(0, 2)
+        def _(group):
+            give(group, 1)
+
+        for below in (True, False):
+            @pl.when(col == (0 if below else 1))
+            def _():
+                for step in range(groups):
+                    edge_copy(step, below, 0, row).wait_recv()
+
+        @pl.loop(2, jnp.where(inner, 4, 3))
+        def _(group):
+            @pl.when(group == NEAR)
+            def _():
+                near_copy(0, row).wait_recv()
+
+            give(group, 0)
+            keep(group, 0)
+            give(group, 1)
+
+        right_copy(1).wait_recv()
+
+        @pl.loop(0, jnp.where(inner, 4, 3))
+        def _(group):
+            keep(group, 1)
+
+    @pl.when(jnp.logical_not(computes))
+    def _():
+        out_ref[...] = jnp.zeros_like(out_ref)
+
+    for source in range(4):
+        far = jnp.abs(row - source)
+
+        @pl.when((far <= 2) & jnp.logical_not(computes & (far == 0)))
+        def _():
+            pltpu.make_async_remote_copy(
+                send_out.at[0, 0], recv_out.at[source], out_send.at[0, 0], out_recv.at[source],
+                device_id={"ka": 1 - ka}, device_id_type=MESH).wait_recv()
+            out_ref[...] += recv_out[source].astype(jnp.float32)
+
+    @pl.when(computes)
+    def _():
+        pair_copy().wait_send()
+        for group in range(4):
+            def done(group=group):
+                for sel in (0, 1):
+                    part_copy(group, sel).wait_send()
+                    if (group, sel) != (OWN, 0):
+                        out_copy(group, sel).wait_send()
+
+            if group == NEAR:
+                pl.when(inner)(done)
+            else:
+                done()
+
+    @pl.when(jnp.logical_not(computes))
+    def _():
+        edges(lambda copy: copy.wait_send())
+        right_copy(0).wait_send()
+        right_copy(1).wait_send()
+
+        @pl.when(inner)
+        def _():
+            near_copy(1 - col, row - toward).wait_send()
+
+
+def fused(left_data, right_data, taper_table, pattern, taper_index):
+    weighted = blend(left_data, taper_table, pattern, taper_index)
+    _, rows, blocks, width = left_data.shape
+    depth = right_data.shape[1] * width
+    sources = right_data.shape[3]
+    panel = weighted.reshape(2, rows, blocks * width // depth, depth).transpose(2, 0, 1, 3)
+    right = right_data.reshape(2, depth, sources)
+    wide = sources // 2
+    dma = pltpu.SemaphoreType.DMA
+    vmem = pl.BlockSpec(memory_space=pltpu.VMEM)
+    return pl.pallas_call(
+        kernel,
+        out_shape=jax.ShapeDtypeStruct((2, rows, wide), jnp.float32),
+        in_specs=[vmem, vmem],
+        out_specs=vmem,
+        scratch_shapes=[
+            pltpu.VMEM((4, 2, rows, depth), jnp.bfloat16),
+            pltpu.VMEM((2, 2, depth, sources), jnp.bfloat16),
+            pltpu.VMEM((4, 2, 2, rows, wide), jnp.float32),
+            pltpu.VMEM((4, 2, 2, rows, wide), jnp.float32),
+            pltpu.VMEM((4, 2, 2, rows, wide), jnp.bfloat16),
+            pltpu.VMEM((4, 2, rows, wide), jnp.bfloat16),
+            dma((2,)), dma((2,)), dma((2,)), dma((8,)), dma((8,)), dma((2,)), dma((2,)),
+            dma((4, 2)), dma((4, 2)), dma((4, 2)), dma((4,)),
+        ],
+        compiler_params=pltpu.CompilerParams(
+            collective_id=0, has_side_effects=True, vmem_limit_bytes=56 * 1024 * 1024
+        ),
+    )(panel, right)
+
+
+def fits(mesh, left_data, right_data, pattern):
+    n_row, n_col, n_ka = mesh.shape["row"], mesh.shape["col"], mesh.shape["ka"]
+    blocks = left_data.shape[2]
+    return (
+        n_row == 4 and n_col == 2 and n_ka == 2 and blocks == 32 and pattern.shape[0] == 2 * blocks
+        and left_data.shape[1] == 1024 and left_data.shape[3] == 256 and right_data.shape[3] == 1024
+    )
+
+
 def solution(mesh):
     placed = (
         P("grp", "row", "col", "ka"),
@@ -60,6 +317,11 @@
         P("row", None),
         P("row", None),
     )
-    return jax.shard_map(
-        local, mesh=mesh, in_specs=placed, out_specs=P("grp", "row", ("col", "ka")), check_vma=False
-    )
+
+    def run(left_data, right_data, taper_table, pattern, taper_index):
+        step = fused if fits(mesh, left_data, right_data, pattern) else local
+        return jax.shard_map(
+            step, mesh=mesh, in_specs=placed, out_specs=P("grp", "row", ("col", "ka")), check_vma=False
+        )(left_data, right_data, taper_table, pattern, taper_index)
+
+    return run

time: 302 us -> 102 us (0.34); the launches traced: 298 us -> 101 us
  waiting for transfers between devices: 257 us -> 0 us
  Pallas kernels: 0 us -> 83 us
  between operations: 13.2 us -> 0.03 us
  matrix products: 9.68 us -> 0.32 us
  local copies, waits for them, and re-layouts: 6.14 us -> 13.6 us
  blocking collectives: 6.48 us -> 0 us
    all_gather x3 -> x0, waiting for transfers between devices: 257 us -> none  [the longest x1 149 us: local(): lax.all_gather(columns, 'row', axis=1, tiled=True)]
    pallas_call x0 -> x1, Pallas kernels: none -> 83 us  [fused(): pl.pallas_call(kernel, out_shape=jax.ShapeDtypeStruct((2, rows, wide), jn...]
    dot_general x1 -> x0, matrix products: 9.36 us -> none  [contract(): jnp.einsum('crjw,djws->cdrs', panel, piece, preferred_element_type=jnp.fl...]
    all_to_all x1 -> x0, blocking collectives: 6.48 us -> none  [local(): lax.all_to_all(right_data, 'ka', split_axis=3, concat_axis=2, tiled=True)]
    reshape x0 -> x1, local copies, waits for them, and re-layouts: none -> 3.99 us  [fused(): weighted.reshape(2, rows, blocks * width // depth, depth)]
    mul x1 -> x2, local copies, waits for them, and re-layouts: 0.15 us -> 3.44 us  [blend(): left_data.astype(jnp.float32)]
    unnamed x5 -> x4, local copies, waits for them, and re-layouts: 3.12 us -> 6.15 us
  transfers between devices with their start and end apart: 3 -> 0, of which waited for: 3 -> 0; matrix products, arithmetic and copies ran while one was open for 2% -> 0% of each run, Pallas kernels for 0% -> 0%
where the time goes in v1:
time: 102 us; the launch traced here: 101 us
  Pallas kernels  83 us (81%)
  local copies, waits for them, and re-layouts  13.6 us (13%)
  other arithmetic  4.37 us (4%)
    pallas_call x1, Pallas kernels, fused(): pl.pallas_call(kernel, out_shape=jax.ShapeDtypeStruct((2, rows, wide), jn...  83 us
    unnamed x4, local copies, waits for them, and re-layouts  6.15 us
    reshape x1, local copies, waits for them, and re-layouts, fused(): weighted.reshape(2, rows, blocks * width // depth, depth)  3.99 us
    convert_element_type x1, other arithmetic, blend(): return shaped.reshape(left_data.shape).astype(jnp.bfloat16)  3.57 us
    mul x2, local copies, waits for them, and re-layouts, blend(): left_data.astype(jnp.float32)  3.44 us

profile of v1, /device:TPU:13, one launch (start us, length us, event | category | flops | bytes accessed | tf_op | source)
XLA Modules:
  0.0 101.3 jit_solution(245763672613704446)
XLA Ops:
  0.0 0.0 copy-start
  0.0 0.8 dynamic-slice_convert_fusion
  0.8 0.0 copy-done
  0.8 0.3 convolution_multiply_fusion
  1.1 1.5 %mul.31 = f32[16,16,16,128]{3,2,1,0:T(8,128)} broadcast(f32[16,16,128]{2,1,0:T(8,128)S(1)} %convolution_multiply_fusion), dimensions={0,2,3} | broadcast | bytes 2228224 | tf_op jit(solution)/shard_map/mul | solution.py:26
  2.6 1.9 %copy.10 = f32[256,16,128]{0,2,1:T(8,128)S(1)} copy(f32[256,16,128]{2,1,0:T(8,128)} %bitcast.8) | data formatting | bytes 4194304 | tf_op jit(solution)/shard_map/mul | solution.py:26
  4.6 4.3 %copy.9 = bf16[2,256,16,128]{1,3,2,0:T(8,128)(2,1)} copy(bf16[2,256,16,128]{3,2,1,0:T(8,128)(2,1)} %param.5) | data formatting | bytes 4194304 | tf_op args[0]
  8.9 3.6 %multiply_convert_fusion = bf16[2,256,16,128]{1,3,2,0:T(8,128)(2,1)} fusion(bf16[2,256,16,128]{1,3,2,0:T(8,128)(2,1)} %copy.9, f32[256,16,128]{0,2,1:T(8,128)S(1)} %copy.10), kind=kLoop, calls=%fused_computation | loop fusion | flops 3145728 | bytes 6291456 | tf_op jit(solution)/shard_map/convert_element_type | solution.py:29
  12.4 4.0 %copy.11 = bf16[2,256,2,1024]{3,1,0,2:T(8,128)(2,1)} copy(bf16[2,256,2,1024]{1,3,2,0:T(8,128)(2,1)} %bitcast.7) | data formatting | bytes 4194304 | tf_op jit(solution)/shard_map/reshape | solution.py:277
  16.4 83.0 %shard_map.55 = f32[2,256,256]{2,1,0:T(8,128)} custom-call(bf16[2,2,256,1024]{3,2,1,0:T(8,128)(2,1)} %bitcast.9, bf16[2,1024,512]{2,1,0:T(8,128)(2,1)} %bitcast.10), custom_call_target="tpu_custom_call" | custom-call | tf_op jit(solution)/shard_map/pallas_call | solution.py:282
  99.4 1.9 %copy.13 = f32[2,256,256]{2,1,0:T(8,128)} copy(f32[2,256,256]{2,1,0:T(8,128)} %shard_map.55) | data formatting | bytes 1048576
Async XLA Ops:
  0.0 0.8 copy-start

commit v2 on v1

v2 whole, which is shorter than its diff:
```python
import jax
import jax.numpy as jnp
from jax import lax
from jax.experimental import pallas as pl
from jax.experimental.pallas import tpu as pltpu
from jax.sharding import PartitionSpec as P


def blend(left_data, taper_table, pattern, taper_index):
    col_part = left_data.shape[2]
    width = left_data.shape[3]
    rows = left_data.shape[1]
    blocks = pattern.shape[0]
    col_start = lax.axis_index("col") * col_part
    ka_start = lax.axis_index("ka") * width
    used = lax.dynamic_slice_in_dim(pattern, col_start, col_part, 1).astype(jnp.float32)
    levels = lax.dynamic_slice_in_dim(taper_index, col_start, col_part, 1)
    table = lax.dynamic_slice_in_dim(taper_table, ka_start, width, 1)
    onehot = (
        levels[:, :, None] == jnp.arange(taper_table.shape[0], dtype=jnp.int32)[None, None, :]
    ).astype(jnp.float32)
    weights = used[:, :, None] * jnp.einsum(
        "bjt,tw->bjw", onehot, table, precision=lax.Precision.HIGHEST
    )
    shaped = (
        left_data.astype(jnp.float32).reshape(2, blocks, rows // blocks, col_part, width)
        * weights[None, :, None]
    )
    return shaped.reshape(left_data.shape).astype(jnp.bfloat16)


def make_step(panel):

    def contract(piece):
        terms = jnp.einsum("crjw,djws->cdrs", panel, piece, preferred_element_type=jnp.float32)
        return jnp.stack([terms[0, 0] - terms[1, 1], terms[0, 1] + terms[1, 0]])

    def step(carry, piece, start):
        return contract(piece)

    return step


def local(left_data, right_data, taper_table, pattern, taper_index):
    weighted = blend(left_data, taper_table, pattern, taper_index)
    rows = left_data.shape[1]
    halves = lax.all_gather(weighted, "ka", axis=3, tiled=True)
    panel = lax.all_gather(halves, "col", axis=2, tiled=True)
    columns = lax.all_to_all(right_data, "ka", split_axis=3, concat_axis=2, tiled=True)
    start_sum = jnp.zeros((2, rows, columns.shape[3]), jnp.float32)
    result = make_step(panel)(
        start_sum, lax.all_gather(columns, "row", axis=1, tiled=True), jnp.int32(0)
    )
    return result


MESH = pl.DeviceIdType.MESH
BAND = 32
THIN = 128
OWN, PAIR, EDGE, NEAR = 0, 1, 2, 3


def weigh(raw, table_ref, pattern_ref, index_ref, turned, weights, loose, panel, col, ka, ready):
    blocks, points = raw.shape[2], raw.shape[3]
    depth = panel.shape[3]
    turned[...] = jnp.zeros_like(turned)
    levels, many = pattern_ref.shape
    turned[0, 0:levels, 0:many] = pattern_ref[...].astype(jnp.float32)
    turned[1, 0:levels, 0:many] = index_ref[...].astype(jnp.float32)
    used = turned[0].T
    level = turned[1].T
    turned[0] = used
    turned[1] = level
    mine = pl.ds(pl.multiple_of(col * blocks, blocks), blocks)
    table = table_ref[:, pl.ds(pl.multiple_of(ka * points, points), points)]
    for block in range(levels):
        column = turned[1, mine, block:block + 1]
        total = jnp.zeros((blocks, points), jnp.float32)
        for tap in range(table.shape[0]):
            total = jnp.where(column == tap, table[tap:tap + 1, :], total)
        weights[block] = total * turned[0, mine, block:block + 1]
    tall = raw.shape[1] // levels
    per = depth // points
    for block in range(levels):
        for part in range(2):
            slot = (2 * block + part) % loose.shape[0]
            rows = slice(block * tall, (block + 1) * tall)
            values = raw[part, rows].astype(jnp.float32) * weights[block][None]
            loose[slot] = values.reshape(tall * blocks, points)
            for j in range(blocks):
                lane = (j % per) * points
                panel[j // per, part, rows, lane:lane + points] = loose[
                    slot, pl.ds(j, tall, stride=blocks), :].astype(jnp.bfloat16)
        if (block + 1) * tall % BAND == 0:
            ready((block + 1) * tall // BAND - 1)


def kernel(left_ref, right_ref, table_ref, pattern_ref, index_ref, out_ref,
           raw, turned, weights, loose, panel, left, rights, part_out, part_in, send_out, recv_out,
           loc_sem, pair_sem, near_sem, edge_send, edge_recv, right_send, right_recv,
           part_send, part_recv, out_send, out_recv):
    row, col, ka = lax.axis_index("row"), lax.axis_index("col"), lax.axis_index("ka")
    side = row // 2
    half = row % 2
    computes = side == col
    idle = jnp.logical_not(computes)
    toward = 1 - 2 * col
    inner = (row == 1) | (row == 2)
    depth = left.shape[3]
    groups = depth // 128
    wide = out_ref.shape[2]

    own_raw = pltpu.make_async_copy(left_ref, raw, loc_sem.at[0])
    own_raw.start()
    left[EDGE] = jnp.zeros(left.shape[1:], left.dtype)

    barrier = pltpu.get_barrier_semaphore()
    for step in range(1, 8):
        to = (row * 2 + col + step) % 8
        pl.semaphore_signal(barrier, inc=1, device_id={"row": to // 2, "col": to % 2}, device_id_type=MESH)
    pl.semaphore_signal(barrier, inc=1, device_id={"ka": 1 - ka}, device_id_type=MESH)
    pl.semaphore_wait(barrier, 8)

    def pair_copy():
        return pltpu.make_async_remote_copy(
            panel.at[1 - half], left.at[PAIR], pair_sem.at[0], pair_sem.at[1],
            device_id={"row": 2 * side + 1 - half}, device_id_type=MESH)

    def near_copy(src_half, to_row):
        return pltpu.make_async_remote_copy(
            panel.at[src_half], left.at[NEAR], near_sem.at[0], near_sem.at[1],
            device_id={"row": to_row}, device_id_type=MESH)

    def edge_copy(step, below, src_half, to_row):
        band = pl.ds(BAND * step, BAND)
        lanes = pl.ds(128 * step, depth - 128 * step) if below else pl.ds(0, 128 * (step + 1))
        return pltpu.make_async_remote_copy(
            panel.at[src_half, :, band, lanes], left.at[EDGE, :, band, lanes],
            edge_send.at[step], edge_recv.at[step],
            device_id={"row": to_row}, device_id_type=MESH)

    def edge(act, step):
        to_row = row - 2 * toward
        for below in (True, False):
            @pl.when(idle & (col == (0 if below else 1)))
            def _():
                act(edge_copy(step, below, to_row % 2, to_row))

    def right_copy(n):
        lanes = pl.ds(THIN * n, THIN)
        return pltpu.make_async_remote_copy(
            right_ref.at[:, :, lanes], rights.at[1, :, :, lanes],
            right_send.at[n], right_recv.at[n],
            device_id={"col": 1 - col}, device_id_type=MESH)

    def own_left():
        return pltpu.make_async_copy(panel.at[half], left.at[OWN], loc_sem.at[0])

    def own_right():
        return pltpu.make_async_copy(right_ref, rights.at[0], loc_sem.at[1])

    @pl.when(idle)
    def _():
        right_copy(0).start()
        right_copy(1).start()

    pl.when(computes)(lambda: own_right().start())

    own_raw.wait()
    weigh(raw, table_ref, pattern_ref, index_ref, turned, weights, loose, panel, col, ka,
          lambda step: edge(lambda copy: copy.start(), step))

    def part_copy(group, sel, start, size):
        here = pl.ds(start % wide, size)
        return pltpu.make_async_remote_copy(
            part_out.at[group, sel, :, :, pl.ds(start, size)], part_in.at[group, sel, :, :, here],
            part_send.at[group, sel, start // size % 2 if sel else 0],
            part_recv.at[group, sel, start // size % 2 if sel else 0],
            device_id={"ka": 1 - ka}, device_id_type=MESH)

    def row_of(group):
        pair = row + 1 - 2 * half
        return jnp.where(group == OWN, row, jnp.where(group == PAIR, pair, jnp.where(
            group == EDGE, row + 2 * toward, row + toward)))

    def out_copy(group, sel, start, size):
        here = pl.ds(start % wide, size)
        to_col = col if sel == 0 else 1 - col
        which = start // size % 2 if sel else 0
        return pltpu.make_async_remote_copy(
            send_out.at[group, sel, :, :, here], recv_out.at[row, :, :, here],
            out_send.at[group, sel, which], out_recv.at[row, which],
            device_id={"row": row_of(group), "col": to_col}, device_id_type=MESH)

    def unit(group, sel, start, size):
        lanes = slice(start, start + size)
        here = slice(start % wide, start % wide + size)
        dot = lambda a, b: jnp.dot(left[group, a], rights[sel, b, :, lanes], preferred_element_type=jnp.float32)
        part_out[group, sel, 0, :, lanes] = dot(0, 0) - dot(1, 1)
        part_out[group, sel, 1, :, lanes] = dot(0, 1) + dot(1, 0)

        @pl.when(ka != start // wide)
        def _():
            part_copy(group, sel, start, size).start()

        @pl.when(ka == start // wide)
        def _():
            part_copy(group, sel, start, size).wait_recv()

            def total():
                return part_out[group, sel, :, :, lanes] + part_in[group, sel, :, :, here]

            def send():
                send_out[group, sel, :, :, here] = total().astype(jnp.bfloat16)
                out_copy(group, sel, start, size).start()

            if sel == 1:
                send()
            else:
                @pl.when(group == OWN)
                def _():
                    out_ref[...] = total()

                pl.when(group != OWN)(send)

    def local_units(group):
        for start in range(0, 2 * wide, wide):
            unit(group, 0, start, wide)

    held = jnp.where(inner, 4, 3)

    @pl.when(computes)
    def _():
        pair_copy().start()
        own_left().start()
        own_right().wait()
        own_left().wait()

        local_units(OWN)
        right_copy(0).wait_recv()
        unit(OWN, 1, 0, THIN)

        pair_copy().wait_recv()
        local_units(PAIR)
        unit(PAIR, 1, 0, THIN)
        right_copy(1).wait_recv()

        @pl.loop(0, 2)
        def _(group):
            unit(group, 1, THIN, THIN)

        for below in (True, False):
            @pl.when(col == (0 if below else 1))
            def _():
                for step in range(groups):
                    edge_copy(step, below, 0, row).wait_recv()

        local_units(EDGE)
        unit(EDGE, 1, 0, THIN)
        unit(EDGE, 1, THIN, THIN)
        right_copy(2).wait_recv()

        @pl.loop(0, 3)
        def _(group):
            unit(group, 1, 2 * THIN, THIN)

        right_copy(3).wait_recv()

        @pl.loop(0, 3)
        def _(group):
            unit(group, 1, 3 * THIN, THIN)

        @pl.when(inner)
        def _():
            near_copy(0, row).wait_recv()
            for n in range(4):
                unit(NEAR, 1, n * THIN, THIN)
            local_units(NEAR)

    @pl.when(idle)
    def _():
        right_copy(0).wait_send()
        right_copy(2).start()
        for step in range(groups):
            edge(lambda copy: copy.wait_send(), step)

        @pl.when(inner)
        def _():
            near_copy(1 - col, row - toward).start()

        right_copy(1).wait_send()
        right_copy(3).start()
        out_ref[...] = jnp.zeros_like(out_ref)

    for source in (0, 3, 1, 2):
        far = jnp.abs(row - source)
        crosses = col != source // 2

        @pl.when((far <= 2) & jnp.logical_not(computes & (far == 0)))
        def _():
            def arrive(which, lanes):
                pltpu.make_async_remote_copy(
                    send_out.at[0, 0, :, :, lanes], recv_out.at[source, :, :, lanes],
                    out_send.at[0, 0, 0], out_recv.at[source, which],
                    device_id={"ka": 1 - ka}, device_id_type=MESH).wait_recv()

            @pl.when(crosses)
            def _():
                arrive(0, pl.ds(0, THIN))
                arrive(1, pl.ds(THIN, THIN))

            @pl.when(jnp.logical_not(crosses))
            def _():
                arrive(0, pl.ds(0, wide))

            out_ref[...] += recv_out[source].astype(jnp.float32)

    @pl.when(computes)
    def _():
        pair_copy().wait_send()
        for group in range(4):
            def done(group=group):
                for sel, size in ((0, wide), (1, THIN)):
                    for start in range(0, 2 * wide, size):
                        @pl.when(ka != start // wide)
                        def _():
                            part_copy(group, sel, start, size).wait_send()

                        if (group, sel) != (OWN, 0):
                            @pl.when(ka == start // wide)
                            def _():
                                out_copy(group, sel, start, size).wait_send()

            if group == NEAR:
                pl.when(inner)(done)
            else:
                done()

    @pl.when(idle)
    def _():
        right_copy(2).wait_send()
        right_copy(3).wait_send()

        @pl.when(inner)
        def _():
            near_copy(1 - col, row - toward).wait_send()


def fused(left_data, right_data, taper_table, pattern, taper_index):
    _, rows, blocks, width = left_data.shape
    depth = right_data.shape[1] * width
    sources = right_data.shape[3]
    right = right_data.reshape(2, depth, sources)
    wide = sources // 2
    dma = pltpu.SemaphoreType.DMA
    vmem, whole = pl.BlockSpec(memory_space=pltpu.VMEM), pl.BlockSpec(memory_space=pl.ANY)
    return pl.pallas_call(
        kernel,
        out_shape=jax.ShapeDtypeStruct((2, rows, wide), jnp.float32),
        in_specs=[whole, whole, vmem, vmem, vmem],
        out_specs=vmem,
        scratch_shapes=[
            pltpu.VMEM(left_data.shape, jnp.bfloat16),
            pltpu.VMEM((2, 128, 128), jnp.float32),
            pltpu.VMEM((pattern.shape[0], blocks, width), jnp.float32),
            pltpu.VMEM((4, rows // pattern.shape[0] * blocks, width), jnp.float32),
            pltpu.VMEM((2, 2, rows, depth), jnp.bfloat16),
            pltpu.VMEM((4, 2, rows, depth), jnp.bfloat16),
            pltpu.VMEM((2, 2, depth, sources), jnp.bfloat16),
            pltpu.VMEM((4, 2, 2, rows, sources), jnp.float32),
            pltpu.VMEM((4, 2, 2, rows, wide), jnp.float32),
            pltpu.VMEM((4, 2, 2, rows, wide), jnp.bfloat16),
            pltpu.VMEM((4, 2, rows, wide), jnp.bfloat16),
            dma((2,)), dma((2,)), dma((2,)), dma((8,)), dma((8,)), dma((4,)), dma((4,)),
            dma((4, 2, 2)), dma((4, 2, 2)), dma((4, 2, 2)), dma((4, 2)),
        ],
        compiler_params=pltpu.CompilerParams(
            collective_id=0, has_side_effects=True, vmem_limit_bytes=60 * 1024 * 1024
        ),
    )(left_data, right, taper_table, pattern, taper_index)


def fits(mesh, left_data, right_data, pattern):
    n_row, n_col, n_ka = mesh.shape["row"], mesh.shape["col"], mesh.shape["ka"]
    blocks = left_data.shape[2]
    return (
        n_row == 4 and n_col == 2 and n_ka == 2 and blocks == 32 and pattern.shape[0] == 2 * blocks
        and left_data.shape[1] == 1024 and left_data.shape[3] == 256 and right_data.shape[3] == 1024
    )


def solution(mesh):
    placed = (
        P("grp", "row", "col", "ka"),
        P("grp", "row", "ka", "col"),
        P(),
        P("row", None),
        P("row", None),
    )

    def run(left_data, right_data, taper_table, pattern, taper_index):
        step = fused if fits(mesh, left_data, right_data, pattern) else local
        return jax.shard_map(
            step, mesh=mesh, in_specs=placed, out_specs=P("grp", "row", ("col", "ka")), check_vma=False
        )(left_data, right_data, taper_table, pattern, taper_index)

    return run
```

time: 102 us -> 83.3 us (0.82)
  local copies, waits for them, and re-layouts: 13.6 us -> 1.87 us
  other arithmetic: 4.37 us -> 0 us
  Pallas kernels: 83 us -> 80.4 us
    convert_element_type x2 -> x0, other arithmetic: 4.37 us -> none  [the longest x1 3.57 us: blend(): return shaped.reshape(left_data.shape).astype(jnp.bfloat16)]
    unnamed x4 -> x1, local copies, waits for them, and re-layouts: 6.15 us -> 1.87 us
    reshape x1 -> x0, local copies, waits for them, and re-layouts: 3.99 us -> none  [fused(): weighted.reshape(2, rows, blocks * width // depth, depth)]
    mul x2 -> x0, local copies, waits for them, and re-layouts: 3.44 us -> none  [blend(): left_data.astype(jnp.float32)]
    pallas_call x1, Pallas kernels: 83 us -> 80.4 us  [fused(): pl.pallas_call(kernel, out_shape=jax.ShapeDtypeStruct((2, rows, wide), jn...]
where the time goes in v2:
time: 83.3 us; the launch traced here: 82.3 us
  Pallas kernels  80.4 us (97%)
  local copies, waits for them, and re-layouts  1.87 us (2%)
    pallas_call x1, Pallas kernels, fused(): pl.pallas_call(kernel, out_shape=jax.ShapeDtypeStruct((2, rows, wide), jn...  80.4 us
    unnamed x1, local copies, waits for them, and re-layouts  1.87 us

profile of v2, /device:TPU:13, one launch (start us, length us, event | category | flops | bytes accessed | tf_op | source)
XLA Modules:
  0.0 82.3 jit_solution(2556877649455309930)
XLA Ops:
  0.0 80.4 %shard_map.55 = f32[2,256,256]{2,1,0:T(8,128)} custom-call(bf16[2,256,16,128]{3,2,1,0:T(8,128)(2,1)} %left_ref.1, bf16[2,1024,512]{2,1,0:T(8,128)(2,1)} %bitcast.1, f32[8,256]{1,0:T(8,128)} %table_ref.1, s32[16,32]{1,0:T(8,128)} %pattern_ref.1, s32[16,32]{1,0:T(8,128)} %index_ref.1), custom_call_target="tpu_custom_call" | custom-call | tf_op jit(solution)/shard_map/pallas_call | solution.py:357
  80.4 1.9 %copy.7 = f32[2,256,256]{2,1,0:T(8,128)} copy(f32[2,256,256]{2,1,0:T(8,128)} %shard_map.55) | data formatting | bytes 1048576

commit v3 on v2

--- a/solution.py
+++ b/solution.py
@@ -97,8 +97,8 @@
 
 def kernel(left_ref, right_ref, table_ref, pattern_ref, index_ref, out_ref,
            raw, turned, weights, loose, panel, left, rights, part_out, part_in, send_out, recv_out,
-           loc_sem, pair_sem, near_sem, edge_send, edge_recv, right_send, right_recv,
-           part_send, part_recv, out_send, out_recv):
+           relay_in, relay_out, loc_sem, pair_sem, near_sem, edge_send, edge_recv, right_send, right_recv,
+           part_send, part_recv, out_send, out_recv, relay_recv, relay_send):
     row, col, ka = lax.axis_index("row"), lax.axis_index("col"), lax.axis_index("ka")
     side = row // 2
     half = row % 2
@@ -192,9 +192,23 @@
             out_send.at[group, sel, which], out_recv.at[row, which],
             device_id={"row": row_of(group), "col": to_col}, device_id_type=MESH)
 
-    def unit(group, sel, start, size):
+    def relay_copy(group, start, size):
+        here = pl.ds(start % wide, size)
+        which = start // size % 2
+        return pltpu.make_async_remote_copy(
+            send_out.at[group, 1, :, :, here], relay_in.at[half, :, :, here],
+            out_send.at[group, 1, which], relay_recv.at[half, which],
+            device_id={"row": row_of(group)}, device_id_type=MESH)
+
+    def forward_copy(which):
+        here = pl.ds(which * THIN, THIN)
+        return pltpu.make_async_remote_copy(
+            relay_out.at[:, :, here], recv_out.at[2 * col, :, :, here],
+            relay_send.at[which], out_recv.at[2 * col, which],
+            device_id={"col": 1 - col}, device_id_type=MESH)
+
+    def multiply(group, sel, start, size):
         lanes = slice(start, start + size)
-        here = slice(start % wide, start % wide + size)
         dot = lambda a, b: jnp.dot(left[group, a], rights[sel, b, :, lanes], preferred_element_type=jnp.float32)
         part_out[group, sel, 0, :, lanes] = dot(0, 0) - dot(1, 1)
         part_out[group, sel, 1, :, lanes] = dot(0, 1) + dot(1, 0)
@@ -203,6 +217,10 @@
         def _():
             part_copy(group, sel, start, size).start()
 
+    def keep(group, sel, start, size):
+        lanes = slice(start, start + size)
+        here = slice(start % wide, start % wide + size)
+
         @pl.when(ka == start // wide)
         def _():
             part_copy(group, sel, start, size).wait_recv()
@@ -215,7 +233,15 @@
                 out_copy(group, sel, start, size).start()
 
             if sel == 1:
-                send()
+                send_out[group, sel, :, :, here] = total().astype(jnp.bfloat16)
+
+                @pl.when(group < EDGE)
+                def _():
+                    out_copy(group, sel, start, size).start()
+
+                @pl.when(group >= EDGE)
+                def _():
+                    relay_copy(group, start, size).start()
             else:
                 @pl.when(group == OWN)
                 def _():
@@ -223,11 +249,9 @@
 
                 pl.when(group != OWN)(send)
 
-    def local_units(group):
+    def local(act, group):
         for start in range(0, 2 * wide, wide):
-            unit(group, 0, start, wide)
-
-    held = jnp.where(inner, 4, 3)
+            act(group, 0, start, wide)
 
     @pl.when(computes)
     def _():
@@ -236,18 +260,26 @@
         own_right().wait()
         own_left().wait()
 
-        local_units(OWN)
+        local(multiply, OWN)
         right_copy(0).wait_recv()
-        unit(OWN, 1, 0, THIN)
+        multiply(OWN, 1, 0, THIN)
+        local(keep, OWN)
 
         pair_copy().wait_recv()
-        local_units(PAIR)
-        unit(PAIR, 1, 0, THIN)
+        local(multiply, PAIR)
+        multiply(PAIR, 1, 0, THIN)
         right_copy(1).wait_recv()
 
         @pl.loop(0, 2)
         def _(group):
-            unit(group, 1, THIN, THIN)
+            multiply(group, 1, THIN, THIN)
+
+        local(keep, PAIR)
+
+        @pl.loop(0, 2)
+        def _(group):
+            keep(group, 1, 0, THIN)
+            keep(group, 1, THIN, THIN)
 
         for below in (True, False):
             @pl.when(col == (0 if below else 1))
@@ -255,27 +287,26 @@
                 for step in range(groups):
                     edge_copy(step, below, 0, row).wait_recv()
 
-        local_units(EDGE)
-        unit(EDGE, 1, 0, THIN)
-        unit(EDGE, 1, THIN, THIN)
-        right_copy(2).wait_recv()
-
-        @pl.loop(0, 3)
-        def _(group):
-            unit(group, 1, 2 * THIN, THIN)
-
-        right_copy(3).wait_recv()
-
-        @pl.loop(0, 3)
-        def _(group):
-            unit(group, 1, 3 * THIN, THIN)
+        for act in (multiply, keep):
+            act(EDGE, 1, 0, THIN)
+            act(EDGE, 1, THIN, THIN)
+            local(act, EDGE)
+
+        for n in (2, 3):
+            right_copy(n).wait_recv()
+
+            for act in (multiply, keep):
+                @pl.loop(0, 3)
+                def _(group, act=act, n=n):
+                    act(group, 1, n * THIN, THIN)
 
         @pl.when(inner)
         def _():
             near_copy(0, row).wait_recv()
-            for n in range(4):
-                unit(NEAR, 1, n * THIN, THIN)
-            local_units(NEAR)
+            for act in (multiply, keep):
+                for n in range(4):
+                    act(NEAR, 1, n * THIN, THIN)
+                local(act, NEAR)
 
     @pl.when(idle)
     def _():
@@ -292,11 +323,42 @@
         right_copy(3).start()
         out_ref[...] = jnp.zeros_like(out_ref)
 
+        for which in range(2):
+            here = slice(which * THIN, (which + 1) * THIN)
+
+            def arrived(index):
+                relay = pltpu.make_async_remote_copy(
+                    relay_out.at[:, :, here], relay_in.at[index, :, :, here],
+                    relay_send.at[which], relay_recv.at[index, which],
+                    device_id={"col": 1 - col}, device_id_type=MESH)
+                relay.wait_recv()
+
+            for near_half in range(2):
+                @pl.when(1 - col == near_half)
+                def _(near_half=near_half):
+                    @pl.when(inner)
+                    def _():
+                        arrived(1 - near_half)
+                        arrived(near_half)
+                        relay_out[:, :, here] = (
+                            relay_in[0, :, :, here].astype(jnp.float32) + relay_in[1, :, :, here].astype(jnp.float32)
+                        ).astype(jnp.bfloat16)
+
+                    @pl.when(jnp.logical_not(inner))
+                    def _():
+                        arrived(near_half)
+                        relay_out[:, :, here] = relay_in[near_half, :, :, here]
+
+            forward_copy(which).start()
+
     for source in (0, 3, 1, 2):
         far = jnp.abs(row - source)
         crosses = col != source // 2
 
-        @pl.when((far <= 2) & jnp.logical_not(computes & (far == 0)))
+        direct = (far <= 2) & jnp.logical_not(computes & (far == 0)) & jnp.logical_not(computes & crosses)
+        relayed = computes & crosses & (source % 2 == 0)
+
+        @pl.when(direct | relayed)
         def _():
             def arrive(which, lanes):
                 pltpu.make_async_remote_copy(
@@ -340,6 +402,8 @@
     def _():
         right_copy(2).wait_send()
         right_copy(3).wait_send()
+        forward_copy(0).wait_send()
+        forward_copy(1).wait_send()
 
         @pl.when(inner)
         def _():
@@ -371,8 +435,10 @@
             pltpu.VMEM((4, 2, 2, rows, wide), jnp.float32),
             pltpu.VMEM((4, 2, 2, rows, wide), jnp.bfloat16),
             pltpu.VMEM((4, 2, rows, wide), jnp.bfloat16),
+            pltpu.VMEM((2, 2, rows, wide), jnp.bfloat16),
+            pltpu.VMEM((2, rows, wide), jnp.bfloat16),
             dma((2,)), dma((2,)), dma((2,)), dma((8,)), dma((8,)), dma((4,)), dma((4,)),
-            dma((4, 2, 2)), dma((4, 2, 2)), dma((4, 2, 2)), dma((4, 2)),
+            dma((4, 2, 2)), dma((4, 2, 2)), dma((4, 2, 2)), dma((4, 2)), dma((2, 2)), dma((2,)),
         ],
         compiler_params=pltpu.CompilerParams(
             collective_id=0, has_side_effects=True, vmem_limit_bytes=60 * 1024 * 1024

time: 83.3 us -> 84.3 us (1.012)
  no operation moved by 1% of the time
where the time goes in v3:
time: 84.3 us; the launch traced here: 83 us
  Pallas kernels  81.2 us (96%)
  local copies, waits for them, and re-layouts  1.87 us (2%)
    pallas_call x1, Pallas kernels, fused(): pl.pallas_call(kernel, out_shape=jax.ShapeDtypeStruct((2, rows, wide), jn...  81.2 us
    unnamed x1, local copies, waits for them, and re-layouts  1.87 us

profile of v3, /device:TPU:13, one launch (start us, length us, event | category | flops | bytes accessed | tf_op | source)
XLA Modules:
  0.0 83.0 jit_solution(4111854430257838121)
XLA Ops:
  0.0 81.2 %shard_map.55 = f32[2,256,256]{2,1,0:T(8,128)} custom-call(bf16[2,256,16,128]{3,2,1,0:T(8,128)(2,1)} %left_ref.1, bf16[2,1024,512]{2,1,0:T(8,128)(2,1)} %bitcast.1, f32[8,256]{1,0:T(8,128)} %table_ref.1, s32[16,32]{1,0:T(8,128)} %pattern_ref.1, s32[16,32]{1,0:T(8,128)} %index_ref.1), custom_call_target="tpu_custom_call" | custom-call | tf_op jit(solution)/shard_map/pallas_call | solution.py:421
  81.2 1.9 %copy.7 = f32[2,256,256]{2,1,0:T(8,128)} copy(f32[2,256,256]{2,1,0:T(8,128)} %shard_map.55) | data formatting | bytes 1048576

commit v4 on v2

--- a/solution.py
+++ b/solution.py
@@ -96,7 +96,7 @@
 
 
 def kernel(left_ref, right_ref, table_ref, pattern_ref, index_ref, out_ref,
-           raw, turned, weights, loose, panel, left, rights, part_out, part_in, send_out, recv_out,
+           raw, turned, weights, loose, panel, left, rights, part_out, given, part_in, send_out, recv_out,
            loc_sem, pair_sem, near_sem, edge_send, edge_recv, right_send, right_recv,
            part_send, part_recv, out_send, out_recv):
     row, col, ka = lax.axis_index("row"), lax.axis_index("col"), lax.axis_index("ka")
@@ -173,7 +173,7 @@
     def part_copy(group, sel, start, size):
         here = pl.ds(start % wide, size)
         return pltpu.make_async_remote_copy(
-            part_out.at[group, sel, :, :, pl.ds(start, size)], part_in.at[group, sel, :, :, here],
+            given.at[group, sel, :, :, pl.ds(start, size)], part_in.at[group, sel, :, :, here],
             part_send.at[group, sel, start // size % 2 if sel else 0],
             part_recv.at[group, sel, start // size % 2 if sel else 0],
             device_id={"ka": 1 - ka}, device_id_type=MESH)
@@ -192,23 +192,27 @@
             out_send.at[group, sel, which], out_recv.at[row, which],
             device_id={"row": row_of(group), "col": to_col}, device_id_type=MESH)
 
-    def unit(group, sel, start, size):
+    def multiply(group, sel, start, size):
         lanes = slice(start, start + size)
-        here = slice(start % wide, start % wide + size)
         dot = lambda a, b: jnp.dot(left[group, a], rights[sel, b, :, lanes], preferred_element_type=jnp.float32)
         part_out[group, sel, 0, :, lanes] = dot(0, 0) - dot(1, 1)
         part_out[group, sel, 1, :, lanes] = dot(0, 1) + dot(1, 0)
 
         @pl.when(ka != start // wide)
         def _():
+            given[group, sel, :, :, lanes] = part_out[group, sel, :, :, lanes].astype(jnp.bfloat16)
             part_copy(group, sel, start, size).start()
 
+    def keep(group, sel, start, size):
+        lanes = slice(start, start + size)
+        here = slice(start % wide, start % wide + size)
+
         @pl.when(ka == start // wide)
         def _():
             part_copy(group, sel, start, size).wait_recv()
 
             def total():
-                return part_out[group, sel, :, :, lanes] + part_in[group, sel, :, :, here]
+                return part_out[group, sel, :, :, lanes] + part_in[group, sel, :, :, here].astype(jnp.float32)
 
             def send():
                 send_out[group, sel, :, :, here] = total().astype(jnp.bfloat16)
@@ -223,11 +227,9 @@
 
                 pl.when(group != OWN)(send)
 
-    def local_units(group):
+    def local(act, group):
         for start in range(0, 2 * wide, wide):
-            unit(group, 0, start, wide)
-
-    held = jnp.where(inner, 4, 3)
+            act(group, 0, start, wide)
 
     @pl.when(computes)
     def _():
@@ -236,18 +238,26 @@
         own_right().wait()
         own_left().wait()
 
-        local_units(OWN)
+        local(multiply, OWN)
         right_copy(0).wait_recv()
-        unit(OWN, 1, 0, THIN)
+        multiply(OWN, 1, 0, THIN)
+        local(keep, OWN)
 
         pair_copy().wait_recv()
-        local_units(PAIR)
-        unit(PAIR, 1, 0, THIN)
+        local(multiply, PAIR)
+        multiply(PAIR, 1, 0, THIN)
         right_copy(1).wait_recv()
 
         @pl.loop(0, 2)
         def _(group):
-            unit(group, 1, THIN, THIN)
+            multiply(group, 1, THIN, THIN)
+
+        local(keep, PAIR)
+
+        @pl.loop(0, 2)
+        def _(group):
+            keep(group, 1, 0, THIN)
+            keep(group, 1, THIN, THIN)
 
         for below in (True, False):
             @pl.when(col == (0 if below else 1))
@@ -255,27 +265,26 @@
                 for step in range(groups):
                     edge_copy(step, below, 0, row).wait_recv()
 
-        local_units(EDGE)
-        unit(EDGE, 1, 0, THIN)
-        unit(EDGE, 1, THIN, THIN)
-        right_copy(2).wait_recv()
-
-        @pl.loop(0, 3)
-        def _(group):
-            unit(group, 1, 2 * THIN, THIN)
-
-        right_copy(3).wait_recv()
-
-        @pl.loop(0, 3)
-        def _(group):
-            unit(group, 1, 3 * THIN, THIN)
+        for act in (multiply, keep):
+            act(EDGE, 1, 0, THIN)
+            act(EDGE, 1, THIN, THIN)
+            local(act, EDGE)
+
+        for n in (2, 3):
+            right_copy(n).wait_recv()
+
+            for act in (multiply, keep):
+                @pl.loop(0, 3)
+                def _(group, act=act, n=n):
+                    act(group, 1, n * THIN, THIN)
 
         @pl.when(inner)
         def _():
             near_copy(0, row).wait_recv()
-            for n in range(4):
-                unit(NEAR, 1, n * THIN, THIN)
-            local_units(NEAR)
+            for act in (multiply, keep):
+                for n in range(4):
+                    act(NEAR, 1, n * THIN, THIN)
+                local(act, NEAR)
 
     @pl.when(idle)
     def _():
@@ -368,7 +377,8 @@
             pltpu.VMEM((4, 2, rows, depth), jnp.bfloat16),
             pltpu.VMEM((2, 2, depth, sources), jnp.bfloat16),
             pltpu.VMEM((4, 2, 2, rows, sources), jnp.float32),
-            pltpu.VMEM((4, 2, 2, rows, wide), jnp.float32),
+            pltpu.VMEM((4, 2, 2, rows, sources), jnp.bfloat16),
+            pltpu.VMEM((4, 2, 2, rows, wide), jnp.bfloat16),
             pltpu.VMEM((4, 2, 2, rows, wide), jnp.bfloat16),
             pltpu.VMEM((4, 2, rows, wide), jnp.bfloat16),
             dma((2,)), dma((2,)), dma((2,)), dma((8,)), dma((8,)), dma((4,)), dma((4,)),

time: 83.3 us -> 83.9 us (level)
  no operation moved by 1% of the time
where the time goes in v4:
time: 83.9 us; the launch traced here: 82.6 us
  Pallas kernels  80.7 us (96%)
  local copies, waits for them, and re-layouts  1.87 us (2%)
    pallas_call x1, Pallas kernels, fused(): pl.pallas_call(kernel, out_shape=jax.ShapeDtypeStruct((2, rows, wide), jn...  80.7 us
    unnamed x1, local copies, waits for them, and re-layouts  1.87 us

profile of v4, /device:TPU:13, one launch (start us, length us, event | category | flops | bytes accessed | tf_op | source)
XLA Modules:
  0.0 82.6 jit_solution(7419360122497231728)
XLA Ops:
  0.0 80.7 %shard_map.55 = f32[2,256,256]{2,1,0:T(8,128)} custom-call(bf16[2,256,16,128]{3,2,1,0:T(8,128)(2,1)} %left_ref.1, bf16[2,1024,512]{2,1,0:T(8,128)(2,1)} %bitcast.1, f32[8,256]{1,0:T(8,128)} %table_ref.1, s32[16,32]{1,0:T(8,128)} %pattern_ref.1, s32[16,32]{1,0:T(8,128)} %index_ref.1), custom_call_target="tpu_custom_call" | custom-call | tf_op jit(solution)/shard_map/pallas_call | solution.py:366
  80.7 1.9 %copy.7 = f32[2,256,256]{2,1,0:T(8,128)} copy(f32[2,256,256]{2,1,0:T(8,128)} %shard_map.55) | data formatting | bytes 1048576
